TPU v7x, 512 devices: a whole 4x8x8 slice. The times are simulated.
512 devices in a mesh: grp: 16 (over z, core), own: 32 (over x, y).
Axes of the slice: x: 4, y: 8, z: 8, core: 2. Of those that a mesh axis runs over, the one named last changes fastest.
Arguments:
- sensitivity: bfloat16 [131072, 64, 128], P(('grp', 'own')), may hold values from -0.75 to 0.75
- residual: bfloat16 [16384, 64], P(('grp', 'own')), may hold values from -6 to 6
- conductivity: float32 [128, 256, 128], P('grp', 'own'), may hold values from -6 to 6
- along_first: float32 [128, 256, 128], P('grp', 'own'), may hold values from 0.3 to 3
- along_second: float32 [128, 256, 128], P('grp', 'own'), may hold values from 0.3 to 3
- along_depth: float32 [128, 256, 128], P('grp', 'own'), may hold values from 0.3 to 3
- sounding: int32 [131072], P(('grp', 'own')), may hold values from 0 to 31
- owner: int32 [131072, 1], P(('grp', 'own')), may hold values from 0 to 31; in each aligned block of 256 rows (0 to 255, 256 to 511, ...) at most 16 rows name the same one
- column: int32 [131072], P(('grp', 'own')), may hold values from 0 to 63
- live_count: int32 [512], P(('grp', 'own')), may hold values from 64 to 256, as said below
Outputs:
- gradient: float32 [128, 256, 128], P('grp', 'own')
Inputs may be any that keep to these rules, and one draw needn't show every extreme that they name: Among the 256 blocks of one device no owner index appears more than 16 times, and in every draw some device has an owner index exactly 16 times. `live_count`: some device has all its 256 blocks live in every draw.
All inputs are finite; a program needn't handle non-finite values.
Results may differ from a plain program's by a relative error of at most 0.0003.
Values sent between devices are 32-bit elements; how exact they have to be, the bound alone decides.
A program may use at most 64 MiB of HBM per device.

v0:
```python
import jax
import jax.numpy as jnp
from jax import lax
from jax.sharding import PartitionSpec as P


def with_halo(cells, sides, width):
    for axis, dim in sides:
        count = lax.axis_size(axis)
        ends = count - 1
        head = lax.slice_in_dim(cells, 0, width, axis=dim)
        tail = lax.slice_in_dim(cells, cells.shape[dim] - width, cells.shape[dim], axis=dim)
        cells = jnp.concatenate(
            [
                lax.ppermute(tail, axis, [(i, (i + 1) % count) for i in range(ends)]),
                cells,
                lax.ppermute(head, axis, [((i + 1) % count, i) for i in range(ends)]),
            ],
            axis=dim,
        )
    return cells


def face_term(extended, weights, start, total, axis):
    size = extended.shape[axis]
    upper = lax.slice_in_dim(extended, 1, size, axis=axis)
    lower = lax.slice_in_dim(extended, 0, size - 1, axis=axis)
    weight_low = lax.slice_in_dim(weights, 0, size - 1, axis=axis)
    position = start - 1 + jnp.arange(size - 1, dtype=jnp.int32)
    valid = (position >= 0) & (position <= total - 2)
    layout = [1, 1, 1]
    layout[axis] = size - 1
    flux = jnp.where(valid.reshape(layout), weight_low * (upper - lower), 0.0)
    return lax.slice_in_dim(flux, 0, size - 2, axis=axis) - lax.slice_in_dim(
        flux, 1, size - 1, axis=axis
    )


def per_device(
    sensitivity,
    residual,
    conductivity,
    along_first,
    along_second,
    along_depth,
    sounding,
    owner,
    column,
    live_count,
):
    blocks = sensitivity.shape[0]
    chosen = jnp.take(residual, sounding, axis=0)
    terms = jnp.einsum("bij,bi->bj", sensitivity, chosen, preferred_element_type=jnp.float32)
    keep = jnp.arange(blocks, dtype=jnp.int32) < live_count[0]
    terms = jnp.where(keep[:, None], terms, 0.0)
    owners = lax.axis_size("own")
    cells_first = conductivity.shape[0]
    cells_second = conductivity.shape[1]
    depth = conductivity.shape[2]
    columns = cells_first * cells_second
    target = owner[:, 0]
    slab_row = (
        jnp.zeros((owners * columns, depth), jnp.float32).at[target * columns + column].add(terms)
    )
    data_part = lax.psum_scatter(slab_row, "own", scatter_dimension=0, tiled=True)
    data_part = data_part.reshape(cells_first, cells_second, depth)
    start_first = lax.axis_index("grp") * cells_first
    total_first = lax.axis_size("grp") * cells_first
    start_second = lax.axis_index("own") * cells_second
    total_second = owners * cells_second
    stacked = jnp.stack([conductivity, along_first, along_second])
    padded = with_halo(stacked, (("grp", 1), ("own", 2)), 1)
    smooth_first = face_term(padded[0][:, 1:-1], padded[1][:, 1:-1], start_first, total_first, 0)
    smooth_second = face_term(padded[0][1:-1, :], padded[2][1:-1, :], start_second, total_second, 1)
    widen = ((0, 0), (0, 0), (1, 1))
    smooth_depth = face_term(jnp.pad(conductivity, widen), jnp.pad(along_depth, widen), 0, depth, 2)
    return data_part + (smooth_first + smooth_second + smooth_depth)


def solution(mesh):
    in_specs = (
        P(("grp", "own"), None, None),
        P(("grp", "own"), None),
        P("grp", "own", None),
        P("grp", "own", None),
        P("grp", "own", None),
        P("grp", "own", None),
        P(("grp", "own")),
        P(("grp", "own"), None),
        P(("grp", "own")),
        P(("grp", "own")),
    )
    out_specs = P("grp", "own", None)
    return jax.shard_map(
        per_device, mesh=mesh, in_specs=in_specs, out_specs=out_specs, check_vma=False
    )
```

profile of v0, /device:TPU:16, one launch (start us, length us, event | category | flops | bytes accessed | tf_op | source)
XLA Modules:
  0.0 248.6 jit_solution(2188830751502629818)
XLA Ops:
  6.5 0.0 copy-start
  6.5 0.0 copy-start.5
  6.5 0.0 copy-start.1
  6.5 0.0 copy-start.3
  6.5 0.0 copy-start.2
  6.5 0.0 copy-start.4
  6.6 0.0 reduce-scatter.2.cloned.1.call-start
  6.6 0.7 compare_select_fusion
  7.3 0.7 compare_and_fusion.3
  8.0 0.7 broadcast_multiply_fusion
  9.4 0.0 copy-done
  9.4 0.9 gather_fusion
  10.2 0.1 select_bitcast_fusion
  10.3 3.4 %fusion.2 = f32[256,1,128]{2,1,0:T(1,128)S(1)} fusion(bf16[256,64,128]{2,1,0:T(8,128)(2,1)} %param.10, bf16[256,64,1]{1,0,2:T(8,128)(2,1)S(1)} %select_bitcast_fusion), kind=kOutput, calls=%fused_computation.5 | convolution fusion | flops 4194304 | bytes 4358144 | tf_op jit(solution)/shard_map/bij,bi->bj/dot_general | solution.py:53
  13.7 0.0 copy-done.5
  13.7 2.5 %scatter_custom_fusion = f32[2048,128]{1,0:T(8,128)} fusion(s32[256]{0:T(256)S(1)} %compare_select_fusion.1, f32[]{:T(128)} %constant.14.clone.1, f32[256,128]{1,0:T(8,128)S(1)} %bitcast.30, pred[256]{0:T(512)(128)(4,1)S(1)} %iota_compare_fusion), kind=kCustom, calls=%fused_computation.2 | custom fusion | flops 65536 | bytes 1181184 | tf_op jit(solution)/shard_map/scatter-add | solution.py:63
  16.2 0.0 reduce-scatter.2.cloned.1.call-update
  16.3 0.0 copy-done.1
  16.3 0.0 copy-done.3
  16.3 0.0 copy-done.2
  16.3 1.7 collective-permute-start
  18.0 1.3 collective-permute-start.1
  19.4 0.0 copy-done.4
  19.4 0.1 fusion.7
  19.5 0.0 collective-permute-done
  19.5 3.8 %collective-permute-done.1 = f32[3,1,8,128]{3,2,1,0:T(8,128)S(1)} collective-permute-done((f32[3,1,8,128]{3,2,1,0:T(8,128)S(1)}, f32[3,1,8,128]{3,2,1,0:T(8,128)S(1)}, u32[]{:S(2)}, u32[]{:S(2)}) %collective-permute-start.1) | collective-permute-done | bytes 12320 | tf_op jit(solution)/shard_map/ppermute | solution.py:17
  23.3 3.5 %collective-permute-start.2 = (f32[3,10,1,128]{3,2,1,0:T(1,128)S(1)}, f32[3,10,1,128]{3,2,1,0:T(1,128)S(1)}, u32[]{:S(2)}, u32[]{:S(2)}) collective-permute-start(f32[3,10,1,128]{3,2,1,0:T(1,128)S(1)} %get-tuple-element.9), channel_id=1, source_target_pairs={{0,1},{1,2},{2,3},{3,4},{4,5},{5,6},{6,7},{7,8},{8,9},{9,10},{10,1... | collective-permute-start | bytes 46088 | tf_op jit(solution)/shard_map/ppermute | solution.py:15
  26.8 2.4 collective-permute-start.3
  29.2 0.0 collective-permute-done.2
  29.2 4.0 %collective-permute-done.3 = f32[3,10,1,128]{3,2,1,0:T(1,128)S(1)} collective-permute-done((f32[3,10,1,128]{3,2,1,0:T(1,128)S(1)}, f32[3,10,1,128]{3,2,1,0:T(1,128)S(1)}, u32[]{:S(2)}, u32[]{:S(2)}) %collective-permute-start.3) | collective-permute-done | bytes 15392 | tf_op jit(solution)/shard_map/ppermute | solution.py:17
  33.2 0.1 pad_maximum_fusion
  33.3 0.1 fusion.13
  33.4 0.1 fusion.9
  33.4 206.9 %reduce-scatter.2.cloned.1.call-done = f32[64,128]{1,0:T(8,128)} async-done(((f32[2048,128]{1,0:T(8,128)}), f32[64,128]{1,0:T(8,128)}) %reduce-scatter.2.cloned.1.call-update) | async-done | bytes 32784 | tf_op jit(solution)/shard_map/reduce_scatter | solution.py:65
  240.3 1.5 fusion.15
  (10 shorter events, 0.1 us)
Async XLA Ops:
  6.5 2.8 %copy-start = (bf16[32,64]{1,0:T(8,128)(2,1)S(1)}, bf16[32,64]{1,0:T(8,128)(2,1)}, u32[]{:S(2)}) copy-start(bf16[32,64]{1,0:T(8,128)(2,1)} %param.11) | copy-start | bytes 12292
  6.5 7.2 %copy-start.5 = (s32[256]{0:T(256)S(1)}, s32[256]{0:T(256)}, u32[]{:S(2)}) copy-start(s32[256]{0:T(256)} %param.18) | copy-start | bytes 3076
  6.5 9.7 %copy-start.1 = (f32[8,8,128]{2,1,0:T(8,128)S(1)}, f32[8,8,128]{2,1,0:T(8,128)}, u32[]{:S(2)}) copy-start(f32[8,8,128]{2,1,0:T(8,128)} %param.12) | copy-start | bytes 98308
  6.5 9.7 %copy-start.3 = (f32[8,8,128]{2,1,0:T(8,128)S(1)}, f32[8,8,128]{2,1,0:T(8,128)}, u32[]{:S(2)}) copy-start(f32[8,8,128]{2,1,0:T(8,128)} %param.13) | copy-start | bytes 98308
  6.5 9.7 %copy-start.2 = (f32[8,8,128]{2,1,0:T(8,128)S(1)}, f32[8,8,128]{2,1,0:T(8,128)}, u32[]{:S(2)}) copy-start(f32[8,8,128]{2,1,0:T(8,128)} %param.14) | copy-start | bytes 98308
  6.5 12.8 %copy-start.4 = (f32[8,8,128]{2,1,0:T(8,128)S(1)}, f32[8,8,128]{2,1,0:T(8,128)}, u32[]{:S(2)}) copy-start(f32[8,8,128]{2,1,0:T(8,128)} %param.15) | copy-start | bytes 98308
  6.6 233.7 %reduce-scatter.2.cloned.1.call-start = ((), (), s32[]{:S(2)}) async-start(), calls=%async_computation.1 | async-start | bytes 1081344 | tf_op jit(solution)/shard_map/reduce_scatter | solution.py:65
  16.3 3.2 %collective-permute-start = (f32[3,1,8,128]{3,2,1,0:T(8,128)S(1)}, f32[3,1,8,128]{3,2,1,0:T(8,128)S(1)}, u32[]{:S(2)}, u32[]{:S(2)}) collective-permute-start(f32[3,1,8,128]{3,2,1,0:T(8,128)S(1)} %get-tuple-element.11), channel_id=1, source_target_pairs={{0,32},{32,64},{64,96},{96,128},{128,160},{160,192},{192,224},{224... | collective-permute-start | bytes 36872 | tf_op jit(solution)/shard_map/ppermute | solution.py:15
  18.0 5.2 %collective-permute-start.1 = (f32[3,1,8,128]{3,2,1,0:T(8,128)S(1)}, f32[3,1,8,128]{3,2,1,0:T(8,128)S(1)}, u32[]{:S(2)}, u32[]{:S(2)}) collective-permute-start(f32[3,1,8,128]{3,2,1,0:T(8,128)S(1)} %get-tuple-element.12), channel_id=1, source_target_pairs={{32,0},{64,32},{96,64},{128,96},{160,128},{192,160},{224,192},{256... | collective-permute-start | bytes 36872 | tf_op jit(solution)/shard_map/ppermute | solution.py:17
  23.3 5.9 %collective-permute-start.2 = (f32[3,10,1,128]{3,2,1,0:T(1,128)S(1)}, f32[3,10,1,128]{3,2,1,0:T(1,128)S(1)}, u32[]{:S(2)}, u32[]{:S(2)}) collective-permute-start(f32[3,10,1,128]{3,2,1,0:T(1,128)S(1)} %get-tuple-element.9), channel_id=1, source_target_pairs={{0,1},{1,2},{2,3},{3,4},{4,5},{5,6},{6,7},{7,8},{8,9},{9,10},{10,1... | collective-permute-start | bytes 46088 | tf_op jit(solution)/shard_map/ppermute | solution.py:15
  26.8 6.4 %collective-permute-start.3 = (f32[3,10,1,128]{3,2,1,0:T(1,128)S(1)}, f32[3,10,1,128]{3,2,1,0:T(1,128)S(1)}, u32[]{:S(2)}, u32[]{:S(2)}) collective-permute-start(f32[3,10,1,128]{3,2,1,0:T(1,128)S(1)} %get-tuple-element.10), channel_id=1, source_target_pairs={{1,0},{2,1},{3,2},{4,3},{5,4},{6,5},{7,6},{8,7},{9,8},{10,9},{11,1... | collective-permute-start | bytes 46088 | tf_op jit(solution)/shard_map/ppermute | solution.py:17
Sparse Core Ops, SparseCore 0:
  16.4 223.8 reduce-scatter.1
where the time goes:
time: 249 us
  waiting for transfers between devices  215 us (86%)
  between operations  14.2 us (6%)
  starting transfers between devices  8.91 us (4%)
  other arithmetic  6.52 us (3%)
  matrix products  3.37 us (1%)
    reduce_scatter x1, waiting for transfers between devices, per_device(): lax.psum_scatter(slab_row, 'own', scatter_dimension=0, tiled=True)  207 us
    ppermute x2, waiting for transfers between devices, with_halo(): lax.ppermute(head, axis, [((i + 1) % count, i) for i in range(ends)])  7.77 us
    ppermute x2, starting transfers between devices, with_halo(): lax.ppermute(tail, axis, [(i, (i + 1) % count) for i in range(ends)])  5.22 us
  transfers between devices with their start and end apart: 5, of which 3 were waited for; matrix products, arithmetic and copies ran while one was open for 0% of the time, Pallas kernels for 0%

commit v1 on v0

v1 whole, which is shorter than its diff:
```python
import functools

import jax
import jax.numpy as jnp
from jax import lax
from jax.experimental import pallas as pl
from jax.experimental.pallas import tpu as pltpu
from jax.sharding import PartitionSpec as P

MESH = pl.DeviceIdType.MESH
CAP = 16
F32 = jnp.float32
BF16 = jnp.bfloat16


def iota(shape, dim):
    return lax.broadcasted_iota(jnp.int32, shape, dim)


def far_first(count):
    return sorted(range(count), key=lambda d: (-min(d, count - d), d))


def split(values):
    high = values.astype(BF16)
    low = (values - high.astype(F32)).astype(BF16)
    return jnp.concatenate([high, low], axis=-1)


def kernel(
    groups,
    xs,
    ys,
    chunks,
    sens_hbm,
    res_hbm,
    model_hbm,
    first_hbm,
    second_hbm,
    depth_hbm,
    sounding_hbm,
    owner_hbm,
    column_hbm,
    live_hbm,
    out_ref,
    sens,
    res,
    field,
    index,
    live,
    terms,
    packed,
    landed,
    tags,
    tags_in,
    halo_first,
    halo_second,
    sens_sem,
    in_sem,
    send_sem,
    recv_sem,
    tag_sem,
    halo_send,
    halo_recv,
):
    owners = xs * ys
    g = lax.axis_index("grp")
    o = lax.axis_index("own")
    x, y = o // ys, o % ys
    blocks = index.shape[2]
    nd = sens.shape[0] // blocks
    lanes = sens.shape[1]
    order = far_first(ys)

    small = [
        pltpu.make_async_copy(owner_hbm, index.at[0], in_sem.at[0]),
        pltpu.make_async_copy(column_hbm, index.at[1], in_sem.at[1]),
        pltpu.make_async_copy(sounding_hbm, index.at[2], in_sem.at[2]),
        pltpu.make_async_copy(live_hbm, live, in_sem.at[3]),
        pltpu.make_async_copy(res_hbm, res, in_sem.at[4]),
    ]
    for copy in small:
        copy.start()
    rows = sens.shape[0] // chunks
    big = [
        pltpu.make_async_copy(
            sens_hbm.at[pl.ds(c * rows, rows)], sens.at[pl.ds(c * rows, rows)], sens_sem.at[c]
        )
        for c in range(chunks)
    ]
    for copy in big:
        copy.start()
    mesh_in = [
        pltpu.make_async_copy(src, field.at[k], in_sem.at[5 + k])
        for k, src in enumerate((model_hbm, first_hbm, second_hbm, depth_hbm))
    ]
    for copy in mesh_in:
        copy.start()

    barrier = pltpu.get_barrier_semaphore()
    around = [
        {"grp": lax.rem(g + 1, groups)},
        {"grp": lax.rem(g + groups - 1, groups)},
    ]
    peers = [None] * owners
    for p in range(ys):
        for dx in range(xs):
            r = p * xs + dx
            peers[r] = {"own": lax.rem(x + dx, xs) * ys + lax.rem(y + order[p], ys)}
    self_slot = order.index(0) * xs
    others = [r for r in range(owners) if r != self_slot]
    for device in around + [peers[r] for r in others]:
        pl.semaphore_signal(barrier, inc=1, device_id=device, device_id_type=MESH)

    for copy in small[:4]:
        copy.wait()
    owner = index[0]
    column = index[1]
    sounding = index[2]
    delta_x = lax.rem(owner // ys - x + xs, xs)
    delta_y = lax.rem(owner % ys - y + ys, ys)
    place = jnp.zeros_like(owner)
    for p in range(ys):
        place = jnp.where(delta_y == order[p], p, place)
    target = place * xs + delta_x
    hot = jnp.where(iota((owners, blocks), 0) == target, 1.0, 0.0)
    before = jnp.where(iota((blocks, blocks), 0) < iota((blocks, blocks), 1), 1.0, 0.0)
    earlier = jnp.dot(hot.astype(BF16), before.astype(BF16), preferred_element_type=F32)
    rank = jnp.sum(hot * earlier, axis=0, keepdims=True).astype(jnp.int32)
    slot = target * CAP + rank

    value = jnp.where(
        lax.rem(iota((lanes, blocks), 0), CAP) == rank, column.astype(F32), 0.0
    )
    tag = lax.dot_general(
        hot.astype(BF16),
        value.astype(BF16),
        (((1,), (1,)), ((), ())),
        preferred_element_type=F32,
    )
    per_row = lanes // CAP
    mine = iota((owners, lanes), 1) // CAP == lax.rem(iota((owners, lanes), 0), per_row)
    tag = jnp.where(mine, tag, 0.0)
    for r in range(owners):
        tags[r] = tag[r : r + 1]
    tags_in[self_slot] = tag[self_slot : self_slot + 1]

    pl.semaphore_wait(barrier, len(around) + len(others))

    halo = []
    for k, (src, dst, device) in enumerate(
        (
            (model_hbm.at[field.shape[1] - 1], halo_first.at[0], around[0]),
            (first_hbm.at[field.shape[1] - 1], halo_first.at[1], around[0]),
            (model_hbm.at[0], halo_first.at[2], around[1]),
            (
                model_hbm.at[:, pl.ds(field.shape[2] - 1, 1)],
                halo_second.at[0],
                {"own": lax.rem(o + 1, owners)},
            ),
            (
                second_hbm.at[:, pl.ds(field.shape[2] - 1, 1)],
                halo_second.at[1],
                {"own": lax.rem(o + 1, owners)},
            ),
            (
                model_hbm.at[:, pl.ds(0, 1)],
                halo_second.at[2],
                {"own": lax.rem(o + owners - 1, owners)},
            ),
        )
    ):
        halo.append(
            pltpu.make_async_remote_copy(
                src_ref=src,
                dst_ref=dst,
                send_sem=halo_send.at[k],
                recv_sem=halo_recv.at[k],
                device_id=device,
                device_id_type=MESH,
            )
        )
    for copy in halo:
        copy.start()

    def tag_copy(first, count, device):
        return pltpu.make_async_remote_copy(
            src_ref=tags.at[pl.ds(first, count)],
            dst_ref=tags_in.at[pl.ds(first, count)],
            send_sem=tag_sem.at[0],
            recv_sem=tag_sem.at[1],
            device_id=device,
            device_id_type=MESH,
        )

    for r in others:
        tag_copy(r, 1, peers[r]).start()

    small[4].wait()
    keep = iota((1, blocks), 1) < live[0]
    picked = jnp.where(
        (iota((res.shape[0], blocks), 0) == sounding) & keep, 1.0, 0.0
    ).astype(BF16)
    twice = jnp.concatenate([res[...]] * (lanes // nd), axis=1)
    chosen = lax.dot_general(
        picked, twice, (((0,), (0,)), ((), ())), preferred_element_type=F32
    ).astype(BF16)
    at_once = 16
    wide = at_once * nd
    diagonal = jnp.where(
        iota((at_once, wide), 0) == iota((at_once, wide), 1) // nd, 1.0, 0.0
    ).astype(BF16)
    done = 0
    for b in range(0, blocks, at_once):
        while done * rows < (b + at_once) * nd:
            big[done].wait()
            done += 1
        left = jnp.concatenate([chosen[b : b + at_once]] * (wide // lanes), axis=1) * diagonal
        part = jnp.dot(left, sens[pl.ds(b * nd, wide)], preferred_element_type=F32)
        terms[pl.ds(b, at_once)] = split(part)

    def packet(first, count, group, device):
        return pltpu.make_async_remote_copy(
            src_ref=packed.at[pl.ds(first, count)],
            dst_ref=landed.at[pl.ds(first, count)],
            send_sem=send_sem.at[0],
            recv_sem=recv_sem.at[group],
            device_id=device,
            device_id_type=MESH,
        )

    step = 2
    for p in range(0, ys, step):
        count = step * xs * CAP
        chosen_rows = jnp.where(
            iota((count, blocks), 0) + p * xs * CAP == slot, 1.0, 0.0
        ).astype(BF16)
        both = jnp.dot(chosen_rows, terms[...], preferred_element_type=F32)
        sums = (both[:, :lanes] + both[:, lanes:]).reshape(step * xs, CAP, lanes)
        packed[pl.ds(p * xs, step * xs)] = sums
        for r in range(p * xs, (p + step) * xs):
            if r != self_slot:
                packet(r, 1, r // xs, peers[r]).start()
            else:
                landed[r] = sums[r - p * xs]

    for copy in mesh_in:
        copy.wait()
    for copy in halo:
        copy.wait()
    model, w1, w2, w3 = field[0], field[1], field[2], field[3]
    cx, cy = field.shape[1], field.shape[2]
    shape = (cx, cy, lanes)

    above = jnp.concatenate([model[1:], halo_first[2][None]], axis=0)
    flux = w1 * (above - model)
    flux = jnp.where((iota(shape, 0) == cx - 1) & (g == groups - 1), 0.0, flux)
    behind = jnp.where(g == 0, 0.0, halo_first[1] * (model[0] - halo_first[0]))
    smooth = jnp.concatenate([behind[None], flux[:-1]], axis=0) - flux

    row = iota(shape, 1)
    above = jnp.where(row == cy - 1, halo_second[2], pltpu.roll(model, cy - 1, 1))
    flux = w2 * (above - model)
    flux = jnp.where((row == cy - 1) & (o == owners - 1), 0.0, flux)
    behind = halo_second[1] * (model[:, 0:1] - halo_second[0])
    behind = jnp.where(o == 0, 0.0, behind)
    smooth = smooth + (jnp.where(row == 0, behind, pltpu.roll(flux, 1, 1)) - flux)

    cell = iota(shape, 2)
    flux = jnp.where(cell == lanes - 1, 0.0, w3 * (pltpu.roll(model, lanes - 1, 2) - model))
    smooth = smooth + (jnp.where(cell == 0, 0.0, pltpu.roll(flux, 1, 2)) - flux)

    tag_copy(0, owners - 1, peers[others[0]]).wait_recv()
    cells = cx * cy
    total = jnp.zeros((cells, 2 * lanes), F32)
    half = owners // 2
    for h in range(2):
        for p in range(h * ys // 2, (h + 1) * ys // 2):
            first, count = p * xs, xs
            if p == self_slot // xs:
                first, count = first + 1, count - 1
            packet(first, count, p, peers[others[0]]).wait_recv()
        names = []
        for q in range(h * half, (h + 1) * half, per_row):
            name = tags_in[q]
            for r in range(q + 1, q + per_row):
                name = name + tags_in[r]
            names.append(name)
        name = jnp.concatenate(names, axis=1).astype(jnp.int32)
        hit = jnp.where(iota((cells, half * CAP), 0) == name, 1.0, 0.0).astype(BF16)
        got = landed[pl.ds(h * half, half)].reshape(half * CAP, lanes)
        total = total + jnp.dot(hit, split(got), preferred_element_type=F32)
    data = (total[:, :lanes] + total[:, lanes:]).reshape(shape)
    out_ref[...] = data + smooth

    tag_copy(0, owners - 1, peers[others[0]]).wait_send()
    packet(0, owners - 1, 0, peers[others[0]]).wait_send()


def solution(mesh):
    groups, owners = mesh.shape["grp"], mesh.shape["own"]
    xs = 4
    ys = owners // xs

    def per_device(sens, res, model, first, second, depth, sounding, owner, column, live):
        blocks, nd, lanes = sens.shape
        cx, cy, _ = model.shape
        chunks = 8
        hbm = pl.BlockSpec(memory_space=pltpu.HBM)
        return pl.pallas_call(
            functools.partial(kernel, groups, xs, ys, chunks),
            out_shape=jax.ShapeDtypeStruct(model.shape, F32),
            in_specs=[hbm] * 10,
            out_specs=pl.BlockSpec(memory_space=pltpu.VMEM),
            scratch_shapes=[
                pltpu.VMEM((blocks * nd, lanes), BF16),
                pltpu.VMEM(res.shape, BF16),
                pltpu.VMEM((4, cx, cy, lanes), F32),
                pltpu.VMEM((3, 1, blocks), jnp.int32),
                pltpu.SMEM((1,), jnp.int32),
                pltpu.VMEM((blocks, 2 * lanes), BF16),
                pltpu.VMEM((owners, CAP, lanes), F32),
                pltpu.VMEM((owners, CAP, lanes), F32),
                pltpu.VMEM((owners, 1, lanes), F32),
                pltpu.VMEM((owners, 1, lanes), F32),
                pltpu.VMEM((3, cy, lanes), F32),
                pltpu.VMEM((3, cx, 1, lanes), F32),
                pltpu.SemaphoreType.DMA((chunks,)),
                pltpu.SemaphoreType.DMA((9,)),
                pltpu.SemaphoreType.DMA((1,)),
                pltpu.SemaphoreType.DMA((ys,)),
                pltpu.SemaphoreType.DMA((2,)),
                pltpu.SemaphoreType.DMA((6,)),
                pltpu.SemaphoreType.DMA((6,)),
            ],
            compiler_params=pltpu.CompilerParams(
                collective_id=0, has_side_effects=True, vmem_limit_bytes=32 * 1024 * 1024
            ),
        )(
            sens.reshape(blocks * nd, lanes),
            res,
            model,
            first,
            second,
            depth,
            sounding.reshape(1, blocks),
            owner.reshape(1, blocks),
            column.reshape(1, blocks),
            live,
        )

    both = ("grp", "own")
    mesh_spec = P("grp", "own", None)
    return jax.shard_map(
        per_device,
        mesh=mesh,
        in_specs=(
            P(both, None, None),
            P(both, None),
            mesh_spec,
            mesh_spec,
            mesh_spec,
            mesh_spec,
            P(both),
            P(both, None),
            P(both),
            P(both),
        ),
        out_specs=mesh_spec,
        check_vma=False,
    )
```

time: 249 us -> 32.4 us (0.13)
  the two profiles are of different devices: /device:TPU:16 before, /device:TPU:8 now
where the time goes in v1:
time: 32.4 us; the launch traced here: 31.9 us
  Pallas kernels  22.6 us (70%)
  local copies, waits for them, and re-layouts  8.56 us (26%)
  between operations  0.68 us (2%)
    pallas_call x1, Pallas kernels, per_device(): pl.pallas_call(functools.partial(kernel, groups, xs, ys, chunks), out_sha...  22.6 us
    unnamed x19, local copies, waits for them, and re-layouts  8.56 us

profile of v1, /device:TPU:8, one launch (start us, length us, event | category | flops | bytes accessed | tf_op | source)
XLA Modules:
  0.0 31.9 jit_solution(14757091863572781448)
XLA Ops:
  0.7 0.0 copy-start
  0.7 2.2 %copy-done = bf16[256,64,128]{2,1,0:T(8,128)(2,1)S(1)} copy-done((bf16[256,64,128]{2,1,0:T(8,128)(2,1)S(1)}, bf16[256,64,128]{2,1,0:T(8,128)(2,1)}, u32[]{:S(2)}) %copy-start) | copy-done | bytes 4194328
  2.8 0.0 copy-start.1
  2.8 0.8 %copy-done.1 = f32[8,8,128]{2,1,0:T(8,128)S(1)} copy-done((f32[8,8,128]{2,1,0:T(8,128)S(1)}, f32[8,8,128]{2,1,0:T(8,128)}, u32[]{:S(2)}) %copy-start.1) | copy-done | bytes 32792
  3.6 0.0 copy-start.2
  3.6 0.8 %copy-done.2 = f32[8,8,128]{2,1,0:T(8,128)S(1)} copy-done((f32[8,8,128]{2,1,0:T(8,128)S(1)}, f32[8,8,128]{2,1,0:T(8,128)}, u32[]{:S(2)}) %copy-start.2) | copy-done | bytes 32792
  4.4 0.0 copy-start.3
  4.4 0.8 %copy-done.3 = f32[8,8,128]{2,1,0:T(8,128)S(1)} copy-done((f32[8,8,128]{2,1,0:T(8,128)S(1)}, f32[8,8,128]{2,1,0:T(8,128)}, u32[]{:S(2)}) %copy-start.3) | copy-done | bytes 32792
  5.1 0.0 copy-start.4
  5.1 0.8 %copy-done.4 = f32[8,8,128]{2,1,0:T(8,128)S(1)} copy-done((f32[8,8,128]{2,1,0:T(8,128)S(1)}, f32[8,8,128]{2,1,0:T(8,128)}, u32[]{:S(2)}) %copy-start.4) | copy-done | bytes 32792
  5.9 0.0 copy-start.5
  5.9 0.7 %copy-done.5 = bf16[32,64]{1,0:T(8,128)(2,1)S(1)} copy-done((bf16[32,64]{1,0:T(8,128)(2,1)S(1)}, bf16[32,64]{1,0:T(8,128)(2,1)}, u32[]{:S(2)}) %copy-start.5) | copy-done | bytes 4120
  6.6 0.0 copy-start.6
  6.6 0.7 %copy-done.6 = s32[256]{0:T(256)S(1)} copy-done((s32[256]{0:T(256)S(1)}, s32[256]{0:T(256)}, u32[]{:S(2)}) %copy-start.6) | copy-done | bytes 1048
  7.3 0.0 copy-start.7
  7.3 0.7 %copy-done.7 = s32[256,1]{0,1:T(1,128)S(1)} copy-done((s32[256,1]{0,1:T(1,128)S(1)}, s32[256,1]{0,1:T(1,128)}, u32[]{:S(2)}) %copy-start.7) | copy-done | bytes 1048
  7.9 0.0 copy-start.8
  7.9 0.7 %copy-done.8 = s32[256]{0:T(256)S(1)} copy-done((s32[256]{0:T(256)S(1)}, s32[256]{0:T(256)}, u32[]{:S(2)}) %copy-start.8) | copy-done | bytes 1048
  8.6 22.6 %shard_map.100 = f32[8,8,128]{2,1,0:T(8,128)S(1)} custom-call(bf16[16384,128]{1,0:T(8,128)(2,1)S(1)} %bitcast.4, bf16[32,64]{1,0:T(8,128)(2,1)S(1)} %copy-done.5, f32[8,8,128]{2,1,0:T(8,128)S(1)} %copy-done.1, f32[8,8,128]{2,1,0:T(8,128)S(1)} %copy-done.2, f32[8,8,128]{2,1,0:T(8,128)S(1)} %copy-done.3, f32[8,8,128]{2,1,0:T(8,128)S(1)} %copy-done.4, ...), custom_call_target="tpu_custom_call" | custom-call | tf_op jit(solution)/shard_map/pallas_call | solution.py:310
  31.3 0.6 %copy.13 = f32[8,8,128]{2,1,0:T(8,128)} copy(f32[8,8,128]{2,1,0:T(8,128)S(1)} %shard_map.100) | data formatting | bytes 65536
Async XLA Ops:
  0.7 2.2 %copy-start = (bf16[256,64,128]{2,1,0:T(8,128)(2,1)S(1)}, bf16[256,64,128]{2,1,0:T(8,128)(2,1)}, u32[]{:S(2)}) copy-start(bf16[256,64,128]{2,1,0:T(8,128)(2,1)} %param.10) | copy-start | bytes 12582916
  2.8 0.8 %copy-start.1 = (f32[8,8,128]{2,1,0:T(8,128)S(1)}, f32[8,8,128]{2,1,0:T(8,128)}, u32[]{:S(2)}) copy-start(f32[8,8,128]{2,1,0:T(8,128)} %model_hbm.1) | copy-start | bytes 98308
  3.6 0.8 %copy-start.2 = (f32[8,8,128]{2,1,0:T(8,128)S(1)}, f32[8,8,128]{2,1,0:T(8,128)}, u32[]{:S(2)}) copy-start(f32[8,8,128]{2,1,0:T(8,128)} %first_hbm.1) | copy-start | bytes 98308
  4.4 0.8 %copy-start.3 = (f32[8,8,128]{2,1,0:T(8,128)S(1)}, f32[8,8,128]{2,1,0:T(8,128)}, u32[]{:S(2)}) copy-start(f32[8,8,128]{2,1,0:T(8,128)} %second_hbm.1) | copy-start | bytes 98308
  5.1 0.8 %copy-start.4 = (f32[8,8,128]{2,1,0:T(8,128)S(1)}, f32[8,8,128]{2,1,0:T(8,128)}, u32[]{:S(2)}) copy-start(f32[8,8,128]{2,1,0:T(8,128)} %depth_hbm.1) | copy-start | bytes 98308
  5.9 0.7 %copy-start.5 = (bf16[32,64]{1,0:T(8,128)(2,1)S(1)}, bf16[32,64]{1,0:T(8,128)(2,1)}, u32[]{:S(2)}) copy-start(bf16[32,64]{1,0:T(8,128)(2,1)} %res_hbm.1) | copy-start | bytes 12292
  6.6 0.7 %copy-start.6 = (s32[256]{0:T(256)S(1)}, s32[256]{0:T(256)}, u32[]{:S(2)}) copy-start(s32[256]{0:T(256)} %param.16) | copy-start | bytes 3076
  7.3 0.7 %copy-start.7 = (s32[256,1]{0,1:T(1,128)S(1)}, s32[256,1]{0,1:T(1,128)}, u32[]{:S(2)}) copy-start(s32[256,1]{0,1:T(1,128)} %param.17) | copy-start | bytes 3076
  7.9 0.7 %copy-start.8 = (s32[256]{0:T(256)S(1)}, s32[256]{0:T(256)}, u32[]{:S(2)}) copy-start(s32[256]{0:T(256)} %param.18) | copy-start | bytes 3076

commit v2 on v1

v2 whole, which is shorter than its diff:
```python
import functools

import jax
import jax.numpy as jnp
from jax import lax
from jax.experimental import pallas as pl
from jax.experimental.pallas import tpu as pltpu
from jax.sharding import PartitionSpec as P

MESH = pl.DeviceIdType.MESH
CAP = 16
F32 = jnp.float32
BF16 = jnp.bfloat16


def iota(shape, dim):
    return lax.broadcasted_iota(jnp.int32, shape, dim)


def rings(count):
    return sorted(range(count), key=lambda d: (min(d, count - d), d))


def split(values):
    high = values.astype(BF16)
    low = (values - high.astype(F32)).astype(BF16)
    return jnp.concatenate([high, low], axis=-1)


def kernel(
    groups,
    xs,
    ys,
    chunks,
    sens_hbm,
    res_hbm,
    model_hbm,
    first_hbm,
    second_hbm,
    depth_hbm,
    sounding_hbm,
    owner_hbm,
    column_hbm,
    live_hbm,
    out_ref,
    sens,
    res,
    field,
    index,
    live,
    terms,
    packed,
    landed,
    halo_first,
    halo_second,
    sens_sem,
    in_sem,
    send_sem,
    recv_sem,
    halo_send,
    halo_recv,
):
    owners = xs * ys
    g = lax.axis_index("grp")
    o = lax.axis_index("own")
    x, y = o // ys, o % ys
    blocks = index.shape[2]
    nd = sens.shape[0] // blocks
    lanes = sens.shape[1]
    order = rings(ys)
    far = y // (ys // 2 + 1)
    me = ((1 - far) * (2 * y - (y + ys - 1) // ys) + far * 2 * (ys - y)) * xs + x

    small = [
        pltpu.make_async_copy(owner_hbm, index.at[0], in_sem.at[0]),
        pltpu.make_async_copy(column_hbm, index.at[1], in_sem.at[1]),
        pltpu.make_async_copy(sounding_hbm, index.at[2], in_sem.at[2]),
        pltpu.make_async_copy(live_hbm, live, in_sem.at[3]),
        pltpu.make_async_copy(res_hbm, res, in_sem.at[4]),
    ]
    for copy in small:
        copy.start()
    rows = sens.shape[0] // chunks
    big = [
        pltpu.make_async_copy(
            sens_hbm.at[pl.ds(c * rows, rows)], sens.at[pl.ds(c * rows, rows)], sens_sem.at[c]
        )
        for c in range(chunks)
    ]
    for copy in big:
        copy.start()
    mesh_in = [
        pltpu.make_async_copy(src, field.at[k], in_sem.at[5 + k])
        for k, src in enumerate((model_hbm, first_hbm, second_hbm, depth_hbm))
    ]
    for copy in mesh_in:
        copy.start()

    peers = [{"own": (k % xs) * ys + order[k // xs]} for k in range(owners)]
    barrier = pltpu.get_barrier_semaphore()
    below, above = {"grp": g - 1}, {"grp": g + 1}

    def tell(semaphore, device):
        pl.semaphore_signal(semaphore, inc=1, device_id=device, device_id_type=MESH)

    for k in range(owners):
        pl.when(k != me)(functools.partial(tell, barrier, peers[k]))
    pl.when(g < groups - 1)(functools.partial(tell, barrier, above))
    pl.when(g > 0)(functools.partial(tell, barrier, below))

    for copy in small[:4]:
        copy.wait()
    owner = index[0]
    column = index[1]
    sounding = index[2]
    row = owner % ys
    row = jnp.where(row > ys // 2, 2 * (ys - row), jnp.maximum(2 * row - 1, 0))
    target = row * xs + owner // ys
    hot = jnp.where(iota((owners, blocks), 0) == target, 1.0, 0.0)
    before = jnp.where(iota((blocks, blocks), 0) < iota((blocks, blocks), 1), 1.0, 0.0)
    earlier = jnp.dot(hot.astype(BF16), before.astype(BF16), preferred_element_type=F32)
    rank = jnp.sum(hot * earlier, axis=0, keepdims=True).astype(jnp.int32)
    slot = target * CAP + rank

    value = jnp.where(
        lax.rem(iota((lanes, blocks), 0), CAP) == rank, column.astype(F32), 0.0
    )
    tag = lax.dot_general(
        hot.astype(BF16),
        value.astype(BF16),
        (((1,), (1,)), ((), ())),
        preferred_element_type=F32,
    )
    per_row = lanes // CAP
    tag = jnp.where(iota((owners, lanes), 1) // CAP == me % per_row, tag, 0.0)
    for k in range(owners):
        packed[k, CAP : CAP + 1] = tag[k : k + 1]

    small[4].wait()
    keep = iota((1, blocks), 1) < live[0]
    picked = jnp.where(
        (iota((res.shape[0], blocks), 0) == sounding) & keep, 1.0, 0.0
    ).astype(BF16)
    twice = jnp.concatenate([res[...]] * (lanes // nd), axis=1)
    chosen = lax.dot_general(
        picked, twice, (((0,), (0,)), ((), ())), preferred_element_type=F32
    ).astype(BF16)
    at_once = 16
    wide = at_once * nd
    diagonal = jnp.where(
        iota((at_once, wide), 0) == iota((at_once, wide), 1) // nd, 1.0, 0.0
    ).astype(BF16)
    done = 0
    for b in range(0, blocks, at_once):
        while done * rows < (b + at_once) * nd:
            big[done].wait()
            done += 1
        left = jnp.concatenate([chosen[b : b + at_once]] * (wide // lanes), axis=1) * diagonal
        part = jnp.dot(left, sens[pl.ds(b * nd, wide)], preferred_element_type=F32)
        terms[pl.ds(b, at_once)] = split(part)

    step = 2 * xs
    for k in range(0, owners, step):
        spots = jnp.where(
            iota((step * CAP, blocks), 0) + k * CAP == slot, 1.0, 0.0
        ).astype(BF16)
        both = jnp.dot(spots, terms[...], preferred_element_type=F32)
        sums = (both[:, :lanes] + both[:, lanes:]).reshape(step, CAP, lanes)
        packed[pl.ds(k, step), pl.ds(0, CAP)] = sums

    def packet(k, count=1):
        return pltpu.make_async_remote_copy(
            src_ref=packed.at[pl.ds(k, count), pl.ds(0, CAP + 1)],
            dst_ref=landed.at[pl.ds(me if count == 1 else k, count), pl.ds(0, CAP + 1)],
            send_sem=send_sem.at[0],
            recv_sem=recv_sem.at[me // per_row],
            device_id=peers[k],
            device_id_type=MESH,
        )

    cx, cy = field.shape[1], field.shape[2]

    def layer(n, src, dst, device):
        return pltpu.make_async_remote_copy(
            src_ref=src,
            dst_ref=dst,
            send_sem=halo_send.at[n],
            recv_sem=halo_recv.at[n],
            device_id=device,
            device_id_type=MESH,
        )

    to_above = [
        layer(0, field.at[0, cx - 1], halo_first.at[0], above),
        layer(1, field.at[1, cx - 1], halo_first.at[1], above),
    ]
    to_below = [layer(2, field.at[0, 0], halo_first.at[2], below)]
    after, ahead = {"own": o + 1}, {"own": o - 1}
    to_after = [
        layer(3, field.at[0, :, pl.ds(cy - 1, 1)], halo_second.at[0], after),
        layer(4, field.at[2, :, pl.ds(cy - 1, 1)], halo_second.at[1], after),
    ]
    to_ahead = [layer(5, field.at[0, :, pl.ds(0, 1)], halo_second.at[2], ahead)]

    def start(copies):
        for copy in copies:
            copy.start()

    def wait_recv(copies):
        for copy in copies:
            copy.wait_recv()

    def wait_send(copies):
        for copy in copies:
            copy.wait_send()

    has_after, has_ahead = o < owners - 1, o > 0
    has_above, has_below = g < groups - 1, g > 0

    for copy in mesh_in:
        copy.wait()
    neighbours = (g + groups - 1) // groups + (2 * groups - 2 - g) // groups
    pl.semaphore_wait(barrier, owners - 1 + neighbours)
    for k in range(owners):
        pl.when(k != me)(lambda k=k: packet(k).start())
    pl.when(has_below)(lambda: start(to_below))
    pl.when(has_above)(lambda: start(to_above))
    pl.when(has_ahead)(lambda: start(to_ahead))
    pl.when(has_after)(lambda: start(to_after))
    landed[pl.ds(me, 1)] = packed[pl.ds(me, 1)]

    pl.when(has_below)(lambda: wait_recv(to_above))
    pl.when(has_above)(lambda: wait_recv(to_below))
    pl.when(has_ahead)(lambda: wait_recv(to_after))
    pl.when(has_after)(lambda: wait_recv(to_ahead))
    model, w1, w2, w3 = field[0], field[1], field[2], field[3]
    shape = (cx, cy, lanes)

    upper = jnp.concatenate([model[1:], halo_first[2][None]], axis=0)
    flux = w1 * (upper - model)
    flux = jnp.where((iota(shape, 0) == cx - 1) & (g == groups - 1), 0.0, flux)
    behind = jnp.where(g == 0, 0.0, halo_first[1] * (model[0] - halo_first[0]))
    smooth = jnp.concatenate([behind[None], flux[:-1]], axis=0) - flux

    row = iota(shape, 1)
    upper = jnp.where(row == cy - 1, halo_second[2], pltpu.roll(model, cy - 1, 1))
    flux = w2 * (upper - model)
    flux = jnp.where((row == cy - 1) & (o == owners - 1), 0.0, flux)
    behind = halo_second[1] * (model[:, 0:1] - halo_second[0])
    behind = jnp.where(o == 0, 0.0, behind)
    smooth = smooth + (jnp.where(row == 0, behind, pltpu.roll(flux, 1, 1)) - flux)

    cell = iota(shape, 2)
    flux = jnp.where(cell == lanes - 1, 0.0, w3 * (pltpu.roll(model, lanes - 1, 2) - model))
    smooth = smooth + (jnp.where(cell == 0, 0.0, pltpu.roll(flux, 1, 2)) - flux)

    cells = cx * cy
    total = jnp.zeros((cells, 2 * lanes), F32)
    for q in range(0, owners, per_row):

        def arrive(count, q=q):
            pltpu.make_async_remote_copy(
                src_ref=packed.at[pl.ds(q, count), pl.ds(0, CAP + 1)],
                dst_ref=landed.at[pl.ds(q, count), pl.ds(0, CAP + 1)],
                send_sem=send_sem.at[0],
                recv_sem=recv_sem.at[q // per_row],
                device_id=peers[0],
                device_id_type=MESH,
            ).wait_recv()

        mine = me // per_row == q // per_row
        pl.when(mine)(lambda: arrive(per_row - 1))
        pl.when(jnp.logical_not(mine))(lambda: arrive(per_row))
        name = landed[q, CAP : CAP + 1]
        for k in range(q + 1, q + per_row):
            name = name + landed[k, CAP : CAP + 1]
        hit = jnp.where(iota((cells, lanes), 0) == name.astype(jnp.int32), 1.0, 0.0).astype(BF16)
        got = landed[pl.ds(q, per_row), pl.ds(0, CAP)].reshape(lanes, lanes)
        total = total + jnp.dot(hit, split(got), preferred_element_type=F32)
    data = (total[:, :lanes] + total[:, lanes:]).reshape(shape)
    out_ref[...] = data + smooth

    packet(0, owners - 1).wait_send()
    pl.when(has_above)(lambda: wait_send(to_above))
    pl.when(has_below)(lambda: wait_send(to_below))
    pl.when(has_after)(lambda: wait_send(to_after))
    pl.when(has_ahead)(lambda: wait_send(to_ahead))


def solution(mesh):
    groups, owners = mesh.shape["grp"], mesh.shape["own"]
    xs = 4
    ys = owners // xs

    def per_device(sens, res, model, first, second, depth, sounding, owner, column, live):
        blocks, nd, lanes = sens.shape
        cx, cy, _ = model.shape
        chunks = 8
        hbm = pl.BlockSpec(memory_space=pltpu.HBM)
        return pl.pallas_call(
            functools.partial(kernel, groups, xs, ys, chunks),
            out_shape=pltpu.VMEM(model.shape, F32),
            in_specs=[hbm] * 10,
            out_specs=pl.BlockSpec(memory_space=pltpu.VMEM),
            scratch_shapes=[
                pltpu.VMEM((blocks * nd, lanes), BF16),
                pltpu.VMEM(res.shape, BF16),
                pltpu.VMEM((4, cx, cy, lanes), F32),
                pltpu.VMEM((3, 1, blocks), jnp.int32),
                pltpu.SMEM((1,), jnp.int32),
                pltpu.VMEM((blocks, 2 * lanes), BF16),
                pltpu.VMEM((owners, CAP + 8, lanes), F32),
                pltpu.VMEM((owners, CAP + 8, lanes), F32),
                pltpu.VMEM((3, cy, lanes), F32),
                pltpu.VMEM((3, cx, 1, lanes), F32),
                pltpu.SemaphoreType.DMA((chunks,)),
                pltpu.SemaphoreType.DMA((9,)),
                pltpu.SemaphoreType.DMA((1,)),
                pltpu.SemaphoreType.DMA((owners // (lanes // CAP),)),
                pltpu.SemaphoreType.DMA((6,)),
                pltpu.SemaphoreType.DMA((6,)),
            ],
            compiler_params=pltpu.CompilerParams(
                collective_id=0, has_side_effects=True, vmem_limit_bytes=60 * 1024 * 1024
            ),
        )(
            sens.reshape(blocks * nd, lanes),
            res,
            model,
            first,
            second,
            depth,
            sounding.reshape(1, blocks),
            owner.reshape(1, blocks),
            column.reshape(1, blocks),
            live,
        )

    both = ("grp", "own")
    mesh_spec = P("grp", "own", None)
    return jax.shard_map(
        per_device,
        mesh=mesh,
        in_specs=(
            P(both, None, None),
            P(both, None),
            mesh_spec,
            mesh_spec,
            mesh_spec,
            mesh_spec,
            P(both),
            P(both, None),
            P(both),
            P(both),
        ),
        out_specs=mesh_spec,
        check_vma=False,
    )
```

time: 32.4 us -> 19.3 us (0.60)
  the two profiles are of different devices: /device:TPU:8 before, /device:TPU:209 now
where the time goes in v2:
time: 19.3 us; the launch traced here: 19.2 us
  Pallas kernels  17.9 us (93%)
  between operations  0.66 us (3%)
  local copies, waits for them, and re-layouts  0.62 us (3%)
    pallas_call x1, Pallas kernels, per_device(): pl.pallas_call(functools.partial(kernel, groups, xs, ys, chunks), out_sha...  17.9 us
    unnamed x1, local copies, waits for them, and re-layouts  0.62 us

profile of v2, /device:TPU:209, one launch (start us, length us, event | category | flops | bytes accessed | tf_op | source)
XLA Modules:
  0.0 19.2 jit_solution(12421789619003454175)
XLA Ops:
  0.7 17.9 %shard_map.100 = f32[8,8,128]{2,1,0:T(8,128)S(1)} custom-call(bf16[16384,128]{1,0:T(8,128)(2,1)} %bitcast.4, bf16[32,64]{1,0:T(8,128)(2,1)} %res_hbm.1, f32[8,8,128]{2,1,0:T(8,128)} %model_hbm.1, f32[8,8,128]{2,1,0:T(8,128)} %first_hbm.1, f32[8,8,128]{2,1,0:T(8,128)} %second_hbm.1, f32[8,8,128]{2,1,0:T(8,128)} %depth_hbm.1, s32[1,256]{1,0:T(1,128)} %bitcast.5, ...), custom_call_target="tpu_custom_call" | custom-call | tf_op jit(solution)/shard_map/pallas_call | solution.py:300
  18.6 0.6 %copy.12 = f32[8,8,128]{2,1,0:T(8,128)} copy(f32[8,8,128]{2,1,0:T(8,128)S(1)} %shard_map.100) | data formatting | bytes 65536

commit v3 on v2

--- a/solution.py
+++ b/solution.py
@@ -59,6 +59,8 @@
     recv_sem,
     halo_send,
     halo_recv,
+    entered,
+    spots,
 ):
     owners = xs * ys
     g = lax.axis_index("grp")
@@ -96,17 +98,45 @@
     for copy in mesh_in:
         copy.start()
 
-    peers = [{"own": (k % xs) * ys + order[k // xs]} for k in range(owners)]
     barrier = pltpu.get_barrier_semaphore()
     below, above = {"grp": g - 1}, {"grp": g + 1}
-
-    def tell(semaphore, device):
-        pl.semaphore_signal(semaphore, inc=1, device_id=device, device_id_type=MESH)
-
-    for k in range(owners):
-        pl.when(k != me)(functools.partial(tell, barrier, peers[k]))
-    pl.when(g < groups - 1)(functools.partial(tell, barrier, above))
-    pl.when(g > 0)(functools.partial(tell, barrier, below))
+    has_after, has_ahead = o < owners - 1, o > 0
+    has_above, has_below = g < groups - 1, g > 0
+    turn = me // xs
+    sides = sorted(range(1, xs), key=lambda d: min(d, xs - d))
+
+    def device(px, py):
+        return {"own": px * ys + py}
+
+    def tell(semaphore, to):
+        pl.semaphore_signal(semaphore, inc=1, device_id=to, device_id_type=MESH)
+
+    late_from = 3
+    late = turn >= late_from
+    early = turn < late_from
+    for dx in sides:
+        tell(barrier, device((x + dx) % xs, y))
+    for p in range(ys):
+
+        def greet(p=p):
+            tell(barrier, device(x, order[p]))
+            if p >= late_from:
+                for dx in sides:
+                    tell(barrier, device((x + dx) % xs, order[p]))
+
+        pl.when(p != turn)(greet)
+    pl.when(has_above)(lambda: tell(barrier, above))
+    with_below = (g + groups - 1) // groups
+
+    def meet_all():
+        pl.semaphore_wait(barrier, owners - 1 + with_below)
+        pl.when(has_below)(lambda: tell(entered.at[0], below))
+
+    def meet():
+        pl.semaphore_wait(barrier, xs - 1 + ys - 1 + with_below)
+        for dx in sides:
+            tell(entered.at[xs - dx], device((x + dx) % xs, y))
+        pl.when(has_below)(lambda: tell(entered.at[0], below))
 
     for copy in small[:4]:
         copy.wait()
@@ -135,6 +165,12 @@
     tag = jnp.where(iota((owners, lanes), 1) // CAP == me % per_row, tag, 0.0)
     for k in range(owners):
         packed[k, CAP : CAP + 1] = tag[k : k + 1]
+
+    at_once = owners // 4
+    for k in range(0, owners, at_once):
+        spots[pl.ds(k * CAP, at_once * CAP)] = jnp.where(
+            iota((at_once * CAP, blocks), 0) + k * CAP == slot, 1.0, 0.0
+        ).astype(BF16)
 
     small[4].wait()
     keep = iota((1, blocks), 1) < live[0]
@@ -159,34 +195,31 @@
         part = jnp.dot(left, sens[pl.ds(b * nd, wide)], preferred_element_type=F32)
         terms[pl.ds(b, at_once)] = split(part)
 
-    step = 2 * xs
+    step = owners // 4
     for k in range(0, owners, step):
-        spots = jnp.where(
-            iota((step * CAP, blocks), 0) + k * CAP == slot, 1.0, 0.0
-        ).astype(BF16)
-        both = jnp.dot(spots, terms[...], preferred_element_type=F32)
+        both = jnp.dot(spots[pl.ds(k * CAP, step * CAP)], terms[...], preferred_element_type=F32)
         sums = (both[:, :lanes] + both[:, lanes:]).reshape(step, CAP, lanes)
         packed[pl.ds(k, step), pl.ds(0, CAP)] = sums
 
-    def packet(k, count=1):
+    def packet(px, p):
         return pltpu.make_async_remote_copy(
-            src_ref=packed.at[pl.ds(k, count), pl.ds(0, CAP + 1)],
-            dst_ref=landed.at[pl.ds(me if count == 1 else k, count), pl.ds(0, CAP + 1)],
+            src_ref=packed.at[pl.ds(p * xs + px, 1), pl.ds(0, CAP + 1)],
+            dst_ref=landed.at[pl.ds(me, 1), pl.ds(0, CAP + 1)],
             send_sem=send_sem.at[0],
             recv_sem=recv_sem.at[me // per_row],
-            device_id=peers[k],
+            device_id=device(px, order[p]),
             device_id_type=MESH,
         )
 
     cx, cy = field.shape[1], field.shape[2]
 
-    def layer(n, src, dst, device):
+    def layer(n, src, dst, to):
         return pltpu.make_async_remote_copy(
             src_ref=src,
             dst_ref=dst,
             send_sem=halo_send.at[n],
             recv_sem=halo_recv.at[n],
-            device_id=device,
+            device_id=to,
             device_id_type=MESH,
         )
 
@@ -214,19 +247,53 @@
         for copy in copies:
             copy.wait_send()
 
-    has_after, has_ahead = o < owners - 1, o > 0
-    has_above, has_below = g < groups - 1, g > 0
-
     for copy in mesh_in:
         copy.wait()
-    neighbours = (g + groups - 1) // groups + (2 * groups - 2 - g) // groups
-    pl.semaphore_wait(barrier, owners - 1 + neighbours)
-    for k in range(owners):
-        pl.when(k != me)(lambda k=k: packet(k).start())
+    pl.when(early)(meet)
+    pl.when(late)(meet_all)
+
+    def send_column(px):
+        for p in [0, 2, 3, 1, 4, 5, 6, 7]:
+            pl.when(p != turn)(lambda p=p: packet(px, p).start())
+
+    def send_row(p):
+        for dx in sides:
+            packet((x + dx) % xs, p).start()
+
+    def send_late():
+        for p in [0, 2, 3, 1, 4, 5, 6, 7]:
+            for px in range(xs):
+                pl.when((p != turn) | (px != x))(lambda p=p, px=px: packet(px, p).start())
+
+    def send_early():
+        send_column(x)
+        for p in range(late_from):
+            pl.when(p == turn)(functools.partial(send_row, p))
+
+    pl.when(late)(send_late)
+    pl.when(early)(send_early)
     pl.when(has_below)(lambda: start(to_below))
-    pl.when(has_above)(lambda: start(to_above))
-    pl.when(has_ahead)(lambda: start(to_ahead))
-    pl.when(has_after)(lambda: start(to_after))
+    pl.when(y > 0)(lambda: start(to_ahead))
+    pl.when(y < ys - 1)(lambda: start(to_after))
+
+    def send_rest():
+        for px in range(xs):
+
+            def column_at(px=px):
+                pl.semaphore_wait(entered.at[(px - x + xs) % xs], 1)
+                send_column(px)
+
+            pl.when(px != x)(column_at)
+
+    pl.when(early)(send_rest)
+    pl.when(has_ahead & (y == 0))(lambda: start(to_ahead))
+    pl.when(has_after & (y == ys - 1))(lambda: start(to_after))
+
+    def tell_above():
+        pl.semaphore_wait(entered.at[0], 1)
+        start(to_above)
+
+    pl.when(has_above)(tell_above)
     landed[pl.ds(me, 1)] = packed[pl.ds(me, 1)]
 
     pl.when(has_below)(lambda: wait_recv(to_above))
@@ -264,7 +331,7 @@
                 dst_ref=landed.at[pl.ds(q, count), pl.ds(0, CAP + 1)],
                 send_sem=send_sem.at[0],
                 recv_sem=recv_sem.at[q // per_row],
-                device_id=peers[0],
+                device_id=after,
                 device_id_type=MESH,
             ).wait_recv()
 
@@ -280,7 +347,14 @@
     data = (total[:, :lanes] + total[:, lanes:]).reshape(shape)
     out_ref[...] = data + smooth
 
-    packet(0, owners - 1).wait_send()
+    pltpu.make_async_remote_copy(
+        src_ref=packed.at[pl.ds(0, owners - 1), pl.ds(0, CAP + 1)],
+        dst_ref=landed.at[pl.ds(0, owners - 1), pl.ds(0, CAP + 1)],
+        send_sem=send_sem.at[0],
+        recv_sem=recv_sem.at[0],
+        device_id=after,
+        device_id_type=MESH,
+    ).wait_send()
     pl.when(has_above)(lambda: wait_send(to_above))
     pl.when(has_below)(lambda: wait_send(to_below))
     pl.when(has_after)(lambda: wait_send(to_after))
@@ -295,7 +369,7 @@
     def per_device(sens, res, model, first, second, depth, sounding, owner, column, live):
         blocks, nd, lanes = sens.shape
         cx, cy, _ = model.shape
-        chunks = 8
+        chunks = 4
         hbm = pl.BlockSpec(memory_space=pltpu.HBM)
         return pl.pallas_call(
             functools.partial(kernel, groups, xs, ys, chunks),
@@ -319,6 +393,8 @@
                 pltpu.SemaphoreType.DMA((owners // (lanes // CAP),)),
                 pltpu.SemaphoreType.DMA((6,)),
                 pltpu.SemaphoreType.DMA((6,)),
+                pltpu.SemaphoreType.REGULAR((xs,)),
+                pltpu.VMEM((owners * CAP, blocks), BF16),
             ],
             compiler_params=pltpu.CompilerParams(
                 collective_id=0, has_side_effects=True, vmem_limit_bytes=60 * 1024 * 1024

time: 19.3 us -> 19.2 us (level)
  the two profiles are of different devices: /device:TPU:209 before, /device:TPU:8 now
where the time goes in v3:
time: 19.2 us; the launch traced here: 19.1 us
  Pallas kernels  17.8 us (93%)
  between operations  0.66 us (3%)
  local copies, waits for them, and re-layouts  0.62 us (3%)
    pallas_call x1, Pallas kernels, per_device(): pl.pallas_call(functools.partial(kernel, groups, xs, ys, chunks), out_sha...  17.8 us
    unnamed x1, local copies, waits for them, and re-layouts  0.62 us

profile of v3, /device:TPU:8, one launch (start us, length us, event | category | flops | bytes accessed | tf_op | source)
XLA Modules:
  0.0 19.1 jit_solution(17296275255741057413)
XLA Ops:
  0.7 17.8 %shard_map.100 = f32[8,8,128]{2,1,0:T(8,128)S(1)} custom-call(bf16[16384,128]{1,0:T(8,128)(2,1)} %bitcast.4, bf16[32,64]{1,0:T(8,128)(2,1)} %res_hbm.1, f32[8,8,128]{2,1,0:T(8,128)} %model_hbm.1, f32[8,8,128]{2,1,0:T(8,128)} %first_hbm.1, f32[8,8,128]{2,1,0:T(8,128)} %second_hbm.1, f32[8,8,128]{2,1,0:T(8,128)} %depth_hbm.1, s32[1,256]{1,0:T(1,128)} %bitcast.5, ...), custom_call_target="tpu_custom_call" | custom-call | tf_op jit(solution)/shard_map/pallas_call | solution.py:374
  18.5 0.6 %copy.12 = f32[8,8,128]{2,1,0:T(8,128)} copy(f32[8,8,128]{2,1,0:T(8,128)S(1)} %shard_map.100) | data formatting | bytes 65536

commit v4 on v3

--- a/solution.py
+++ b/solution.py
@@ -112,28 +112,52 @@
         pl.semaphore_signal(semaphore, inc=1, device_id=to, device_id_type=MESH)
 
     late_from = 3
-    late = turn >= late_from
-    early = turn < late_from
-    for dx in sides:
-        tell(barrier, device((x + dx) % xs, y))
-    for p in range(ys):
-
-        def greet(p=p):
-            tell(barrier, device(x, order[p]))
-            if p >= late_from:
-                for dx in sides:
-                    tell(barrier, device((x + dx) % xs, order[p]))
-
-        pl.when(p != turn)(greet)
+    herald = 2
+    first = g == 0
+    origin = first & (o == 0)
+    late = (turn >= late_from) | (first & (turn == 0))
+    early = jnp.logical_not(late)
+    with_below = (g + groups - 1) // groups
+    is_herald = 1 - ((o - herald) * (o - herald) + owners * owners - 1) // (owners * owners)
+    is_origin = 1 - (o + owners - 1) // owners
+    without = (1 - with_below) * (1 - is_herald) * (1 - is_origin)
+
+    def greet_row(p):
+        for dx in sides:
+            tell(barrier, device((x + dx) % xs, order[p]))
+
+    def greet_all():
+        for dx in sides:
+            tell(barrier, device((x + dx) % xs, y))
+        for p in range(ys):
+
+            def greet(p=p):
+                tell(barrier, device(x, order[p]))
+                if p >= late_from:
+                    greet_row(p)
+                elif p == 0:
+                    pl.when(first)(lambda: greet_row(0))
+
+            pl.when(p != turn)(greet)
+
+    pl.when(jnp.logical_not(origin))(greet_all)
+    pl.when(origin)(lambda: tell(barrier, device(0, herald)))
     pl.when(has_above)(lambda: tell(barrier, above))
-    with_below = (g + groups - 1) // groups
+
+    def announce():
+        for p in range(ys):
+            for px in range(xs):
+                if px * ys + order[p] not in (0, herald):
+                    tell(entered.at[xs], device(px, order[p]))
 
     def meet_all():
-        pl.semaphore_wait(barrier, owners - 1 + with_below)
+        pl.semaphore_wait(barrier, owners - 1 + with_below - without)
         pl.when(has_below)(lambda: tell(entered.at[0], below))
+        pl.when(first & (o == herald))(announce)
 
     def meet():
-        pl.semaphore_wait(barrier, xs - 1 + ys - 1 + with_below)
+        in_column = 1 - (x + xs - 1) // xs
+        pl.semaphore_wait(barrier, xs - 1 + ys - 1 + with_below - (1 - with_below) * in_column)
         for dx in sides:
             tell(entered.at[xs - dx], device((x + dx) % xs, y))
         pl.when(has_below)(lambda: tell(entered.at[0], below))
@@ -252,18 +276,27 @@
     pl.when(early)(meet)
     pl.when(late)(meet_all)
 
+    hold = first & (o != herald)
+    sequence = [p for p in (0, 2, 3, 1, 4, 5, 6, 7) if p < ys]
+
     def send_column(px):
-        for p in [0, 2, 3, 1, 4, 5, 6, 7]:
-            pl.when(p != turn)(lambda p=p: packet(px, p).start())
+        for p in sequence:
+            go = p != turn
+            if p == 0:
+                go = go & jnp.logical_not(hold & (px == 0))
+            pl.when(go)(lambda p=p: packet(px, p).start())
 
     def send_row(p):
         for dx in sides:
             packet((x + dx) % xs, p).start()
 
     def send_late():
-        for p in [0, 2, 3, 1, 4, 5, 6, 7]:
+        for p in sequence:
             for px in range(xs):
-                pl.when((p != turn) | (px != x))(lambda p=p, px=px: packet(px, p).start())
+                go = (p != turn) | (px != x)
+                if p == 0 and px == 0:
+                    go = go & jnp.logical_not(hold)
+                pl.when(go)(lambda p=p, px=px: packet(px, p).start())
 
     def send_early():
         send_column(x)
@@ -273,7 +306,7 @@
     pl.when(late)(send_late)
     pl.when(early)(send_early)
     pl.when(has_below)(lambda: start(to_below))
-    pl.when(y > 0)(lambda: start(to_ahead))
+    pl.when((y > 0) & jnp.logical_not(first & (o == 1)))(lambda: start(to_ahead))
     pl.when(y < ys - 1)(lambda: start(to_after))
 
     def send_rest():
@@ -288,6 +321,13 @@
     pl.when(early)(send_rest)
     pl.when(has_ahead & (y == 0))(lambda: start(to_ahead))
     pl.when(has_after & (y == ys - 1))(lambda: start(to_after))
+
+    def send_origin():
+        pl.semaphore_wait(entered.at[xs], 1)
+        packet(0, 0).start()
+        pl.when(o == 1)(lambda: start(to_ahead))
+
+    pl.when(hold & (o != 0))(send_origin)
 
     def tell_above():
         pl.semaphore_wait(entered.at[0], 1)
@@ -393,7 +433,7 @@
                 pltpu.SemaphoreType.DMA((owners // (lanes // CAP),)),
                 pltpu.SemaphoreType.DMA((6,)),
                 pltpu.SemaphoreType.DMA((6,)),
-                pltpu.SemaphoreType.REGULAR((xs,)),
+                pltpu.SemaphoreType.REGULAR((xs + 1,)),
                 pltpu.VMEM((owners * CAP, blocks), BF16),
             ],
             compiler_params=pltpu.CompilerParams(

time: 19.2 us -> 18 us (0.938)
  Pallas kernels: 17.8 us -> 16.6 us
    pallas_call x1, Pallas kernels: 17.8 us -> 16.6 us  [per_device(): pl.pallas_call(functools.partial(kernel, groups, xs, ys, chunks), out_sha...]
where the time goes in v4:
time: 18 us; the launch traced here: 17.9 us
  Pallas kernels  16.6 us (92%)
  between operations  0.66 us (4%)
  local copies, waits for them, and re-layouts  0.62 us (3%)
    pallas_call x1, Pallas kernels, per_device(): pl.pallas_call(functools.partial(kernel, groups, xs, ys, chunks), out_sha...  16.6 us
    unnamed x1, local copies, waits for them, and re-layouts  0.62 us

profile of v4, /device:TPU:8, one launch (start us, length us, event | category | flops | bytes accessed | tf_op | source)
XLA Modules:
  0.0 17.9 jit_solution(1744420374377772853)
XLA Ops:
  0.7 16.6 %shard_map.100 = f32[8,8,128]{2,1,0:T(8,128)S(1)} custom-call(bf16[16384,128]{1,0:T(8,128)(2,1)} %bitcast.4, bf16[32,64]{1,0:T(8,128)(2,1)} %res_hbm.1, f32[8,8,128]{2,1,0:T(8,128)} %model_hbm.1, f32[8,8,128]{2,1,0:T(8,128)} %first_hbm.1, f32[8,8,128]{2,1,0:T(8,128)} %second_hbm.1, f32[8,8,128]{2,1,0:T(8,128)} %depth_hbm.1, s32[1,256]{1,0:T(1,128)} %bitcast.5, ...), custom_call_target="tpu_custom_call" | custom-call | tf_op jit(solution)/shard_map/pallas_call | solution.py:414
  17.3 0.6 %copy.12 = f32[8,8,128]{2,1,0:T(8,128)} copy(f32[8,8,128]{2,1,0:T(8,128)S(1)} %shard_map.100) | data formatting | bytes 65536

commit v5 on v4

--- a/solution.py
+++ b/solution.py
@@ -291,12 +291,12 @@
             packet((x + dx) % xs, p).start()
 
     def send_late():
-        for p in sequence:
-            for px in range(xs):
-                go = (p != turn) | (px != x)
-                if p == 0 and px == 0:
-                    go = go & jnp.logical_not(hold)
-                pl.when(go)(lambda p=p, px=px: packet(px, p).start())
+        places = [(px, p) for half in (range(2), range(2, xs)) for p in sequence[:4] for px in half] + [(px, p) for p in sequence[4:] for px in range(xs)]
+        for px, p in places:
+            go = (p != turn) | (px != x)
+            if p == 0 and px == 0:
+                go = go & jnp.logical_not(hold)
+            pl.when(go)(lambda p=p, px=px: packet(px, p).start())
 
     def send_early():
         send_column(x)

time: 18 us -> 18 us (level)
  the two profiles are of different devices: /device:TPU:8 before, /device:TPU:142 now
where the time goes in v5:
time: 18 us; the launch traced here: 17.9 us
  Pallas kernels  16.6 us (92%)
  between operations  0.66 us (4%)
  local copies, waits for them, and re-layouts  0.62 us (3%)
    pallas_call x1, Pallas kernels, per_device(): pl.pallas_call(functools.partial(kernel, groups, xs, ys, chunks), out_sha...  16.6 us
    unnamed x1, local copies, waits for them, and re-layouts  0.62 us

profile of v5, /device:TPU:142, one launch (start us, length us, event | category | flops | bytes accessed | tf_op | source)
XLA Modules:
  0.0 17.9 jit_solution(13549202211389128358)
XLA Ops:
  0.7 16.6 %shard_map.100 = f32[8,8,128]{2,1,0:T(8,128)S(1)} custom-call(bf16[16384,128]{1,0:T(8,128)(2,1)} %bitcast.4, bf16[32,64]{1,0:T(8,128)(2,1)} %res_hbm.1, f32[8,8,128]{2,1,0:T(8,128)} %model_hbm.1, f32[8,8,128]{2,1,0:T(8,128)} %first_hbm.1, f32[8,8,128]{2,1,0:T(8,128)} %second_hbm.1, f32[8,8,128]{2,1,0:T(8,128)} %depth_hbm.1, s32[1,256]{1,0:T(1,128)} %bitcast.5, ...), custom_call_target="tpu_custom_call" | custom-call | tf_op jit(solution)/shard_map/pallas_call | solution.py:414
  17.2 0.6 %copy.12 = f32[8,8,128]{2,1,0:T(8,128)} copy(f32[8,8,128]{2,1,0:T(8,128)S(1)} %shard_map.100) | data formatting | bytes 65536

commit v6 on v5

--- a/solution.py
+++ b/solution.py
@@ -277,7 +277,7 @@
     pl.when(late)(meet_all)
 
     hold = first & (o != herald)
-    sequence = [p for p in (0, 2, 3, 1, 4, 5, 6, 7) if p < ys]
+    sequence = [p for p in (0, 1, 3, 2, 4, 5, 6, 7) if p < ys]
 
     def send_column(px):
         for p in sequence:

time: 18 us -> 17.6 us (0.978)
  the two profiles are of different devices: /device:TPU:142 before, /device:TPU:446 now
where the time goes in v6:
time: 17.6 us; the launch traced here: 17.5 us
  Pallas kernels  16.2 us (92%)
  between operations  0.66 us (4%)
  local copies, waits for them, and re-layouts  0.62 us (4%)
    pallas_call x1, Pallas kernels, per_device(): pl.pallas_call(functools.partial(kernel, groups, xs, ys, chunks), out_sha...  16.2 us
    unnamed x1, local copies, waits for them, and re-layouts  0.62 us

profile of v6, /device:TPU:446, one launch (start us, length us, event | category | flops | bytes accessed | tf_op | source)
XLA Modules:
  0.0 17.5 jit_solution(3958493749185698273)
XLA Ops:
  0.7 16.2 %shard_map.100 = f32[8,8,128]{2,1,0:T(8,128)S(1)} custom-call(bf16[16384,128]{1,0:T(8,128)(2,1)} %bitcast.4, bf16[32,64]{1,0:T(8,128)(2,1)} %res_hbm.1, f32[8,8,128]{2,1,0:T(8,128)} %model_hbm.1, f32[8,8,128]{2,1,0:T(8,128)} %first_hbm.1, f32[8,8,128]{2,1,0:T(8,128)} %second_hbm.1, f32[8,8,128]{2,1,0:T(8,128)} %depth_hbm.1, s32[1,256]{1,0:T(1,128)} %bitcast.5, ...), custom_call_target="tpu_custom_call" | custom-call | tf_op jit(solution)/shard_map/pallas_call | solution.py:414
  16.9 0.6 %copy.12 = f32[8,8,128]{2,1,0:T(8,128)} copy(f32[8,8,128]{2,1,0:T(8,128)S(1)} %shard_map.100) | data formatting | bytes 65536
